TPU v7x, 256 devices: a whole 4x4x8 slice. The times are simulated.
256 devices in a mesh: ctx: 32 (over y, x, core), tp: 8 (over z).
Axes of the slice: x: 4, y: 4, z: 8, core: 2. Of those that a mesh axis runs over, the one named last changes fastest.
Arguments:
- query_rows: bfloat16 [1, 32, 512, 4096], P(None, 'ctx', None, 'tp'), may hold values from -200 to 200
- key_rows: bfloat16 [1, 32, 512, 1024], P(None, 'ctx', None, 'tp'), may hold values from -8 to 8
- value_rows: bfloat16 [1, 32, 512, 1024], P(None, 'ctx', None, 'tp'), may hold values from -12 to 12
- block_choice: int32 [1, 32, 512, 8, 3], P(None, 'ctx', None, 'tp'), may hold values from 0 to 31, as said below
- out_weight: bfloat16 [4096, 4096], P('tp'), may hold values from -0.1875 to 0.1875
- residual: bfloat16 [1, 32, 512, 4096], P(None, 'ctx', 'tp'), may hold values from -3 to 3
Outputs:
- mixed: bfloat16 [1, 32, 512, 4096], P(None, 'ctx', 'tp')
Inputs may be any that keep to these rules, and one draw needn't show every extreme that they name: `block_choice`: entry 0 is the token's own block; block s lies on device s % 32. For one device and key head, its tokens form groups of 128 consecutive tokens that share entries 1 and 2. Each of these entries names an earlier block or repeats the token's own block (which then adds nothing). No other device is named by more than one group and entry of the same device and key head, so at most 128 tokens of one device and key head read blocks on any one other device, and exactly 128 do for some pair in every draw.
All inputs are finite; a program needn't handle non-finite values.
Results may differ from a plain program's by a relative error of at most 0.015.
Values may be sent and summed in bfloat16 or wider, within the bound.
A program may use at most 128 MiB of HBM per device.

v0:
```python
import math

import jax
import jax.numpy as jnp
from jax import lax
from jax.sharding import PartitionSpec as P

H = 32
KVH = 8
HD = 128


def soft_pool(scores, allowed, value_block, pattern):
    masked = jnp.where(allowed, scores, -jnp.inf)
    peak = jnp.max(masked, axis=-1, keepdims=True)
    safe_peak = jnp.where(jnp.isfinite(peak), peak, 0.0)
    weights = jnp.where(allowed, jnp.exp(masked - safe_peak), 0.0)
    total = jnp.sum(weights, axis=-1, keepdims=True)
    safe_total = jnp.where(total > 0.0, total, 1.0)
    pooled = jnp.einsum(
        pattern, weights.astype(jnp.bfloat16), value_block, preferred_element_type=jnp.float32
    )
    return (pooled / safe_total, (safe_peak + jnp.log(safe_total))[..., 0])


def body(query_rows, key_rows, value_rows, block_choice, out_weight, residual):
    slot_count = query_rows.shape[0]
    block_len = query_rows.shape[2]
    head_width = query_rows.shape[3]
    kv_here = key_rows.shape[3] // HD
    group_size = H // KVH
    group_width = group_size * HD
    scaling = 1.0 / math.sqrt(HD)
    ctx_size = lax.axis_size("ctx")
    ctx_index = lax.axis_index("ctx")
    local_rows = slot_count * block_len
    query_view = query_rows.reshape(slot_count, block_len, kv_here, group_size, HD)
    key_view = key_rows.reshape(slot_count, block_len, kv_here, HD)
    value_view = value_rows.reshape(slot_count, block_len, kv_here, HD)
    positions = jnp.arange(block_len)
    causal = (positions[:, None] >= positions[None, :])[None, :, None, None, :]
    own_scores = (
        jnp.einsum("snkgd,smkd->snkgm", query_view, key_view, preferred_element_type=jnp.float32)
        * scaling
    )
    own_pooled, own_logsum = soft_pool(own_scores, causal, value_view, "snkgm,smkd->snkgd")
    own_block = jnp.arange(slot_count, dtype=jnp.int32)[:, None, None] * ctx_size + ctx_index
    chosen = block_choice[:, 0, :, :, 1:]
    usable = chosen != own_block[..., None]
    entry_dev = jnp.moveaxis(chosen % ctx_size, 3, 0)
    entry_slot = jnp.moveaxis(chosen // ctx_size, 3, 0)
    entry_usable = jnp.moveaxis(usable, 3, 0)
    key_slot = jnp.arange(local_rows, dtype=jnp.int32) // block_len
    key_flat = key_rows[:, 0].reshape(local_rows, kv_here, HD)
    value_flat = value_rows[:, 0].reshape(local_rows, kv_here, HD)
    capacity = block_len // 4
    slot_total = ctx_size * kv_here * capacity
    kv_ids = jnp.arange(kv_here, dtype=jnp.int32)
    pair_flat = (entry_dev * kv_here + kv_ids).reshape(-1)
    slot_flat = entry_slot.reshape(-1)
    usable_flat = entry_usable.reshape(-1)
    pair_ids = jnp.arange(ctx_size * kv_here, dtype=jnp.int32)
    onehot = ((pair_flat[:, None] == pair_ids[None, :]) & usable_flat[:, None]).astype(jnp.int32)
    ranking = jnp.sum((jnp.cumsum(onehot, axis=0) - 1) * onehot, axis=1)
    placing = jnp.where(usable_flat, pair_flat * capacity + ranking, slot_total)
    query_flat = query_rows[:, 0].reshape(local_rows * kv_here, group_width)
    sent_rows = jnp.broadcast_to(query_flat[None], (2,) + query_flat.shape).reshape(-1, group_width)
    row_buffer = (
        jnp.zeros((slot_total, group_width), jnp.bfloat16).at[placing].set(sent_rows, mode="drop")
    )
    slot_buffer = jnp.full((slot_total,), -1, jnp.int32).at[placing].set(slot_flat, mode="drop")
    row_send = row_buffer.reshape(ctx_size, kv_here, capacity, group_width)
    slot_send = slot_buffer.reshape(ctx_size, kv_here, capacity)
    got_rows = lax.all_to_all(row_send, "ctx", split_axis=0, concat_axis=0, tiled=True)
    got_slots = lax.all_to_all(slot_send, "ctx", split_axis=0, concat_axis=0, tiled=True)
    row_count = got_rows.shape[2]
    tile_span = 1
    while (
        tile_span * 2 <= ctx_size
        and ctx_size % (tile_span * 2) == 0
        and (tile_span * 2 * row_count * kv_here <= 512)
    ):
        tile_span = tile_span * 2
    tile_count = ctx_size // tile_span
    tile_rows = got_rows.reshape(tile_count, tile_span, kv_here, row_count, group_size, HD)
    tile_slots = got_slots.reshape(tile_count, tile_span, kv_here, row_count)

    def one_tile(packed):
        rows_now, slots_now = packed
        scores = (
            jnp.einsum("skrgd,mkd->skrgm", rows_now, key_flat, preferred_element_type=jnp.float32)
            * scaling
        )
        allowed = (slots_now[..., None] == key_slot)[:, :, :, None, :]
        return soft_pool(scores, allowed, value_flat, "skrgm,mkd->skrgd")

    pooled, logsum = lax.map(one_tile, (tile_rows, tile_slots))
    pooled_all = pooled.reshape(ctx_size, kv_here, row_count, group_width)
    logsum_all = logsum.reshape(ctx_size, kv_here, row_count, group_size)
    pooled_back = lax.all_to_all(pooled_all, "ctx", split_axis=0, concat_axis=0, tiled=True)
    logsum_back = lax.all_to_all(logsum_all, "ctx", split_axis=0, concat_axis=0, tiled=True)
    clipped = jnp.minimum(placing, slot_total - 1)
    flat_pooled = pooled_back.reshape(slot_total, group_size, HD)[clipped]
    flat_logsum = logsum_back.reshape(slot_total, group_size)[clipped]
    flat_logsum = jnp.where(usable_flat[:, None], flat_logsum, -jnp.inf)
    far_pooled = flat_pooled.reshape(2, slot_count, block_len, kv_here, group_size, HD)
    far_logsum = flat_logsum.reshape(2, slot_count, block_len, kv_here, group_size)
    top_logsum = jnp.maximum(own_logsum, jnp.max(far_logsum, axis=0))
    own_scale = jnp.exp(own_logsum - top_logsum)
    far_scale = jnp.exp(far_logsum - top_logsum)
    numerator = own_scale[..., None] * own_pooled + jnp.sum(
        far_scale[..., None] * far_pooled, axis=0
    )
    denominator = own_scale + jnp.sum(far_scale, axis=0)
    attention = (
        (numerator / denominator[..., None])
        .astype(jnp.bfloat16)
        .reshape(slot_count, block_len, head_width)
    )
    tp_size = lax.axis_size("tp")
    share = block_len // tp_size
    ordered = (
        attention.reshape(slot_count, tp_size, share, head_width)
        .transpose(1, 0, 2, 3)
        .reshape(tp_size * slot_count * share, head_width)
    )
    rows_now = ordered
    summed = lax.psum_scatter(
        jnp.dot(rows_now, out_weight, preferred_element_type=jnp.float32).astype(jnp.bfloat16),
        "tp",
        scatter_dimension=0,
        tiled=True,
    ).astype(jnp.float32)
    model_width = out_weight.shape[1]
    mixed = summed + residual.reshape(slot_count * share, model_width).astype(jnp.float32)
    return mixed.astype(jnp.bfloat16).reshape(slot_count, 1, share, model_width)


def solution(mesh):
    placed = (
        P(None, "ctx", None, "tp"),
        P(None, "ctx", None, "tp"),
        P(None, "ctx", None, "tp"),
        P(None, "ctx", None, "tp", None),
        P("tp", None),
        P(None, "ctx", "tp", None),
    )
    return jax.shard_map(
        body, mesh=mesh, in_specs=placed, out_specs=P(None, "ctx", "tp", None), check_vma=False
    )
```

profile of v0, /device:TPU:24, one launch (start us, length us, event | category | flops | bytes accessed | tf_op | source)
XLA Modules:
  0.0 379.4 jit_solution(10213249482011064091)
XLA Ops:
  8.0 9.0 %reduce-window.6 = s32[32,8,128]{2,1,0:T(8,128)S(1)} reduce-window(s32[32,8,128]{2,1,0:T(8,128)S(1)} %fusion.55, s32[]{:T(128)} %copy.123), window={size=1x1x128 pad=0_0x0_0x127_0}, to_apply=%region_2.3 | reduce-window | flops 4161536 | bytes 262148 | tf_op jit(solution)/shard_map/reduce-window
  18.7 7.7 %scatter_custom_fusion.1 = bf16[4096,512]{1,0:T(8,128)(2,1)} fusion(s32[1024]{0:T(1024)S(1)} %bitcast.253, bf16[1024,512]{1,0:T(8,128)(2,1)S(1)} %bitcast.236, bf16[]{:T(256)} %constant.89.clone.1), kind=kCustom, calls=%fused_computation.49 | custom fusion | bytes 4194306 | tf_op jit(solution)/shard_map/scatter | solution.py:69
  26.5 7.4 %all-to-all-start.1 = ((bf16[32,1,128,512]{3,2,1,0:T(8,128)(2,1)}), bf16[32,1,128,512]{3,2,1,0:T(8,128)(2,1)}, u32[]{:S(2)}, u32[]{:S(2)}) async-start(bf16[32,1,128,512]{3,2,1,0:T(8,128)(2,1)} %bitcast.226), calls=%async_computation.1 | async-start | bytes 8388608 | tf_op jit(solution)/shard_map/all_to_all | solution.py:74
  33.9 4.9 %scatter_custom_fusion = s32[4096]{0:T(1024)} fusion(s32[1024]{0:T(1024)S(1)} %bitcast.254, s32[1024]{0:T(1024)S(1)} %bitcast.252, s32[]{:T(128)} %constant.93.clone.1), kind=kCustom, calls=%fused_computation.87 | custom fusion | bytes 16388 | tf_op jit(solution)/shard_map/scatter | solution.py:71
  38.8 45.5 %all-to-all-done.1 = bf16[32,1,128,512]{3,2,1,0:T(8,128)(2,1)} async-done(((bf16[32,1,128,512]{3,2,1,0:T(8,128)(2,1)}), bf16[32,1,128,512]{3,2,1,0:T(8,128)(2,1)}, u32[]{:S(2)}, u32[]{:S(2)}) %all-to-all-start.1) | async-done | bytes 4194336 | tf_op jit(solution)/shard_map/all_to_all | solution.py:74
  84.3 7.0 %all-to-all-start = ((s32[32,1,128]{2,1,0:T(1,128)}), s32[32,1,128]{2,1,0:T(1,128)S(1)}, u32[]{:S(2)}, u32[]{:S(2)}) async-start(s32[32,1,128]{2,1,0:T(1,128)} %bitcast.17), calls=%async_computation | async-start | bytes 32768 | tf_op jit(solution)/shard_map/all_to_all | solution.py:75
  91.3 6.5 %copy.72 = bf16[32,1,128,512]{2,3,0,1:T(8,128)(2,1)} copy(bf16[32,1,128,512]{3,2,1,0:T(8,128)(2,1)} %all-to-all-done.1) | data formatting | bytes 8388608 | tf_op jit(solution)/shard_map/all_to_all | solution.py:74
  97.8 55.7 %while.13 = (s32[]{:T(128)}, f32[8,4,1,128,4,128]{3,5,4,1,0,2:T(8,128)}, f32[8,4,1,128,4]{3,4,1,2,0:T(4,128)S(1)}, s32[8,4,1,128]{3,1,2,0:T(4,128)S(1)}, bf16[8,...) while((s32[]{:T(128)}, ...), condition=%wide.region_10.11_spmd.clone, body=%wide.region_7.10_spmd.clone.sunk | while | flops 551045120 | bytes 19770460 | solution.py:97
  105.0 2.0 fusion.72
  112.0 2.0 fusion.72
  118.9 2.0 fusion.72
  132.8 2.0 fusion.72
  139.8 2.0 fusion.72
  153.5 12.8 %all_to_all.20 = f32[32,1,128,4]{2,3,1,0:T(4,128)S(1)} all-to-all(f32[32,1,128,4]{2,3,1,0:T(4,128)S(1)} %bitcast.239), channel_id=1, replica_groups=mesh['ctx'=32,'tp'=8] {'ctx'}, dimensions={0} | all-to-all | bytes 131072 | tf_op jit(solution)/shard_map/all_to_all | solution.py:101
  166.2 6.9 %all-to-all-start.3 = ((f32[32,1,128,512]{2,3,1,0:T(8,128)}), f32[32,1,128,512]{2,3,1,0:T(8,128)}, u32[]{:S(2)}, u32[]{:S(2)}) async-start(f32[32,1,128,512]{2,3,1,0:T(8,128)} %bitcast.229), calls=%async_computation.3 | async-start | bytes 16777216 | tf_op jit(solution)/shard_map/all_to_all | solution.py:100
  178.2 2.8 gather_fusion
  182.9 91.5 %all-to-all-done.3 = f32[32,1,128,512]{2,3,1,0:T(8,128)} async-done(((f32[32,1,128,512]{2,3,1,0:T(8,128)}), f32[32,1,128,512]{2,3,1,0:T(8,128)}, u32[]{:S(2)}, u32[]{:S(2)}) %all-to-all-start.3) | async-done | bytes 8388640 | tf_op jit(solution)/shard_map/all_to_all | solution.py:100
  274.3 9.0 %copy.92 = f32[32,1,128,512]{3,2,0,1:T(8,128)} copy(f32[32,1,128,512]{2,3,1,0:T(8,128)} %all-to-all-done.3) | data formatting | bytes 16777216 | tf_op jit(solution)/shard_map/reshape | solution.py:103
  283.3 9.9 %reshape.655 = f32[4096,4,128]{2,1,0:T(4,128)} reshape(f32[32,1,128,512]{3,2,0,1:T(8,128)} %copy.92) | data formatting | bytes 16777216 | tf_op jit(solution)/shard_map/reshape | solution.py:103
  293.3 6.9 %gather_fusion.1 = f32[1024,4,128]{2,1,0:T(4,128)S(1)} fusion(f32[4096,4,128]{2,1,0:T(4,128)} %reshape.655, s32[1024]{0:T(1024)S(1)} %broadcast_clamp_fusion), kind=kCustom, calls=%fused_computation.1 | custom fusion | bytes 4198400 | tf_op jit(solution)/shard_map/gather | solution.py:103
  300.2 4.1 %multiply_reduce_fusion = f32[512,4,128]{2,1,0:T(4,128)S(1)} fusion(f32[2,1,512,1,4,128]{5,4,2,0,3,1:T(4,128)S(1)} %bitcast.228, f32[2,512,4]{2,1,0:T(8,128)} %subtract_exponential_fusion), kind=kLoop, calls=%fused_computation.48 | loop fusion | flops 786432 | bytes 3162112 | tf_op jit(solution)/shard_map/reduce_sum | solution.py:111
  304.6 3.5 fusion.43
  308.1 4.3 %convolution_convert_fusion = bf16[512,4096]{1,0:T(8,128)(2,1)} fusion(bf16[512,512]{0,1:T(8,128)(2,1)S(1)} %bitcast.237, bf16[512,4096]{1,0:T(8,128)(2,1)S(1)} %copy-done.2), kind=kOutput, calls=%fused_computation.41 | convolution fusion | flops 2149580800 | bytes 8912896 | tf_op jit(solution)/shard_map/dot_general | solution.py:129
  312.5 58.1 %reduce-scatter.2.cloned.1.call-done = bf16[64,4096]{1,0:T(8,128)(2,1)} async-done(((bf16[512,4096]{1,0:T(8,128)(2,1)}), bf16[64,4096]{1,0:T(8,128)(2,1)}) %reduce-scatter.2.cloned.1.call-update) | async-done | bytes 524304 | tf_op jit(solution)/shard_map/reduce_scatter | solution.py:128
  (133 shorter events, 57.3 us)
Async XLA Ops:
  26.5 57.8 %all-to-all-start.1 = ((bf16[32,1,128,512]{3,2,1,0:T(8,128)(2,1)}), bf16[32,1,128,512]{3,2,1,0:T(8,128)(2,1)}, u32[]{:S(2)}, u32[]{:S(2)}) async-start(bf16[32,1,128,512]{3,2,1,0:T(8,128)(2,1)} %bitcast.226), calls=%async_computation.1 | async-start | bytes 8388608 | tf_op jit(solution)/shard_map/all_to_all | solution.py:74
  84.3 13.5 %all-to-all-start = ((s32[32,1,128]{2,1,0:T(1,128)}), s32[32,1,128]{2,1,0:T(1,128)S(1)}, u32[]{:S(2)}, u32[]{:S(2)}) async-start(s32[32,1,128]{2,1,0:T(1,128)} %bitcast.17), calls=%async_computation | async-start | bytes 32768 | tf_op jit(solution)/shard_map/all_to_all | solution.py:75
  91.3 6.5 %copy-start.1 = (bf16[1,1,512,128]{3,2,1,0:T(8,128)(2,1)S(1)}, bf16[1,1,512,128]{3,2,1,0:T(8,128)(2,1)}, u32[]{:S(2)}) copy-start(bf16[1,1,512,128]{3,2,1,0:T(8,128)(2,1)} %param.9) | copy-start | bytes 393220
  91.3 6.5 %copy-start.5 = (bf16[1,1,512,128]{3,2,1,0:T(8,128)(2,1)S(1)}, bf16[1,1,512,128]{3,2,1,0:T(8,128)(2,1)}, u32[]{:S(2)}) copy-start(bf16[1,1,512,128]{3,2,1,0:T(8,128)(2,1)} %param.10) | copy-start | bytes 393220
  166.2 7.2 %copy-start.3 = (bf16[1,1,512,512]{3,2,1,0:T(8,128)(2,1)S(1)}, bf16[1,1,512,512]{3,2,1,0:T(8,128)(2,1)}, u32[]{:S(2)}) copy-start(bf16[1,1,512,512]{3,2,1,0:T(8,128)(2,1)} %param.8) | copy-start | bytes 1572868
  166.2 108.1 %all-to-all-start.3 = ((f32[32,1,128,512]{2,3,1,0:T(8,128)}), f32[32,1,128,512]{2,3,1,0:T(8,128)}, u32[]{:S(2)}, u32[]{:S(2)}) async-start(f32[32,1,128,512]{2,3,1,0:T(8,128)} %bitcast.229), calls=%async_computation.3 | async-start | bytes 16777216 | tf_op jit(solution)/shard_map/all_to_all | solution.py:100
  173.2 197.4 %reduce-scatter.2.cloned.1.call-start = ((), (), s32[]{:S(2)}) async-start(), calls=%async_computation.5 | async-start | bytes 4718592 | tf_op jit(solution)/shard_map/reduce_scatter | solution.py:128
  174.5 1.9 copy-start
  304.6 3.5 copy-start.2
  312.4 58.2 %copy-start.4 = (bf16[1,1,64,4096]{3,2,1,0:T(8,128)(2,1)S(1)}, bf16[1,1,64,4096]{3,2,1,0:T(8,128)(2,1)}, u32[]{:S(2)}) copy-start(bf16[1,1,64,4096]{3,2,1,0:T(8,128)(2,1)} %param.13) | copy-start | bytes 1572868
Sparse Core Ops, SparseCore 0:
  312.6 57.9 reduce-scatter.1
where the time goes:
time: 382 us; the launch traced here: 379 us
  waiting for transfers between devices  195 us (51%)
  local copies, waits for them, and re-layouts  64 us (17%)
  matrix products  39 us (10%)
  other arithmetic  32.8 us (9%)
  starting transfers between devices  21.5 us (6%)
  between operations  13.7 us (4%)
  blocking collectives  12.8 us (3%)
    all_to_all x1, waiting for transfers between devices, body(): lax.all_to_all(pooled_all, 'ctx', split_axis=0, concat_axis=0, tiled=True)  91.5 us
    reduce_scatter x1, waiting for transfers between devices, body(): lax.psum_scatter(jnp.dot(rows_now, out_weight, preferred_element_type=jnp...  58.1 us
    all_to_all x1, waiting for transfers between devices, body(): lax.all_to_all(row_send, 'ctx', split_axis=0, concat_axis=0, tiled=True)  45.5 us
    reshape x2, local copies, waits for them, and re-layouts, body(): flat_pooled = pooled_back.reshape(slot_total, group_size, HD)[clipped]  18.9 us
    dot_general x9, matrix products, soft_pool(): jnp.einsum(pattern, weights.astype(jnp.bfloat16), value_block, preferred_...  17.6 us
    dot_general x8, matrix products, one_tile(): jnp.einsum('skrgd,mkd->skrgm', rows_now, key_flat, preferred_element_type...  16.2 us
    all_to_all x1, blocking collectives, body(): lax.all_to_all(logsum_all, 'ctx', split_axis=0, concat_axis=0, tiled=True)  12.8 us
    reduce_sum x9, other arithmetic, soft_pool(): total = jnp.sum(weights, axis=-1, keepdims=True)  12.6 us
  transfers between devices with their start and end apart: 4, of which 3 were waited for; matrix products, arithmetic and copies ran while one was open for 5% of the time, Pallas kernels for 0%

commit v1 on v0

v1 whole, which is shorter than its diff:
```python
import functools
import math

import jax
import jax.numpy as jnp
from jax import lax
from jax.experimental import pallas as pl
from jax.experimental.pallas import tpu as pltpu
from jax.sharding import PartitionSpec as P

MESH = pl.DeviceIdType.MESH
HD = 128
HEADS = 4
BLK = 512
NX, NY, NZ = 4, 4, 8
WIDTH = 4096
HALF = 2048
QUART = 1024
CHUNKS = 8
NEG = -1e30
EXP2 = math.log2(math.e) / math.sqrt(HD)


def kernel(
    choice, q_ref, k_ref, v_ref, w_hbm, res_ref, out_ref,
    kv, w, own_acc, own_max, own_sum, att_send, att_in, part, rin0, rin, fin_send, fin_in,
    w_sem, y_send, y_recv, x_send, x_recv, a_send, a_recv, r_send, r_recv, f_send, f_recv,
):
    c = lax.axis_index("ctx")
    z = lax.axis_index("tp")
    core = lax.rem(c, 2)
    x = lax.rem(c // 2, NX)
    y = c // (2 * NX)

    def index(xx, yy, cc):
        return (yy * NX + xx) * 2 + cc

    x_next, x_prev = lax.rem(x + 1, NX), lax.rem(x + NX - 1, NX)
    x_far = lax.rem(x + 2, NX)
    right = (index(x_next, y, core), z)
    left = (index(x_prev, y, core), z)
    sibling = (index(x, y, 1 - core), z)
    up = (c, lax.rem(z + 1, NZ))
    down = (c, lax.rem(z + NZ - 1, NZ))

    def row(yy):
        return (index(x, yy, core), z)

    def remote(src, dst, s_sem, r_sem, device):
        return pltpu.make_async_remote_copy(
            src_ref=src, dst_ref=dst, send_sem=s_sem, recv_sem=r_sem, device_id=device, device_id_type=MESH
        )

    barrier = pltpu.get_barrier_semaphore()
    for device in (right, left, sibling, up, down):
        pl.semaphore_signal(barrier, inc=1, device_id=device, device_id_type=MESH)
    for step in range(1, NY):
        pl.semaphore_signal(barrier, inc=1, device_id=row(lax.rem(y + step, NY)), device_id_type=MESH)
    w_copy = pltpu.make_async_copy(w_hbm, w, w_sem)
    w_copy.start()
    kv[c, 0] = k_ref[...]
    kv[c, 1] = v_ref[...]
    pl.semaphore_wait(barrier, 8)

    def y_copy(step):
        target = lax.rem(y + step, NY)
        return remote(kv.at[c], kv.at[c], y_send.at[step - 1], y_recv.at[y], row(target))

    def y_arrival(layer):
        b = index(x, layer, core)
        return remote(kv.at[b], kv.at[b], y_send.at[0], y_recv.at[layer], row(lax.rem(y + 1, NY)))

    def blocks(j, cc):
        layer = y - j
        return [index(xx, layer, cc) for xx in (x, x_prev, x_next, x_far)]

    def x_copy(j, n, src, device):
        return remote(src, src, x_send.at[j, n], x_recv.at[j, n], device)

    def x_send_copy(j, n):
        mine, prev, nxt, far = blocks(j, core)
        src = [kv.at[mine], kv.at[mine], kv.at[mine], kv.at[prev, 0], kv.at[nxt, 1],
               kv.at[prev], kv.at[nxt], kv.at[far]][n]
        return x_copy(j, n, src, [right, left, sibling, right, left, sibling, sibling, sibling][n])

    def x_arrival(j, n):
        mine, prev, nxt, far = blocks(j, core)
        s_mine, s_prev, s_nxt, s_far = blocks(j, 1 - core)
        ref = [kv.at[prev], kv.at[nxt], kv.at[s_mine], kv.at[far, 0], kv.at[far, 1],
               kv.at[s_prev], kv.at[s_nxt], kv.at[s_far]][n]
        return x_copy(j, n, ref, sibling)

    def gather_0(j):
        @pl.when((j >= 0) & (j <= y))
        def _():
            @pl.when(j >= 1)
            def _():
                y_arrival(y - j).wait_recv()
            for n in (0, 1, 2):
                x_send_copy(j, n).start()

    def gather_1(j):
        @pl.when((j >= 0) & (j <= y))
        def _():
            x_arrival(j, 0).wait_recv()
            x_send_copy(j, 3).start()
            x_send_copy(j, 5).start()
            x_arrival(j, 1).wait_recv()
            x_send_copy(j, 4).start()
            x_send_copy(j, 6).start()

    def gather_2(j):
        @pl.when((j >= 0) & (j <= y))
        def _():
            x_arrival(j, 3).wait_recv()
            x_arrival(j, 4).wait_recv()
            x_send_copy(j, 7).start()

    def gather(n):
        gather_1(n - 1)
        gather_0(n)
        gather_2(n - 2)

    gather_0(jnp.int32(0))
    for step in range(1, NY):
        @pl.when(y + step < NY)
        def _():
            y_copy(step).start()

    def stacked(r, g):
        rows = []
        for h in range(HEADS):
            for u in (2 * g, 2 * g + 1):
                start = pl.multiple_of(64 * u + 16 * r, 16)
                rows.append(q_ref[pl.ds(start, 16), h * HD:(h + 1) * HD])
        return jnp.concatenate(rows, axis=0)

    def scores(qs, keys):
        return lax.dot_general(qs, keys, (((1,), (1,)), ((), ())), preferred_element_type=jnp.float32)

    def own_quarter(r, carry):
        for g in range(4):
            keys = 128 * (g + 1)
            s = scores(stacked(r, g), k_ref[0:keys, :])
            a = lax.broadcasted_iota(jnp.int32, (128, keys), 0)
            token = 128 * g + 64 * (lax.rem(a, 32) // 16) + 16 * r + lax.rem(a, 16)
            key = lax.broadcasted_iota(jnp.int32, (128, keys), 1)
            s = jnp.where(key <= token, s, NEG)
            m = jnp.max(s, axis=1, keepdims=True)
            p = jnp.exp2((s - m) * EXP2)
            n = r * 4 + g
            own_max[n] = m
            own_sum[n] = jnp.sum(p, axis=1, keepdims=True)
            own_acc[n] = jnp.dot(p.astype(jnp.bfloat16), v_ref[0:keys, :], preferred_element_type=jnp.float32)
        return carry

    lax.fori_loop(0, 4, own_quarter, 0)

    def a_copy(r):
        return remote(att_send.at[r], att_in.at[y], a_send.at[r], a_recv.at[y], row(r))

    def a_arrival(k):
        return remote(att_in.at[k], att_in.at[k], a_send.at[0], a_recv.at[k], row(lax.rem(y + 1, NY)))

    def far_attention():
        def wait_layer(j, carry):
            for n in (2, 5, 6, 7):
                x_arrival(j, n).wait_recv()
            return carry

        lax.fori_loop(0, y + 1, wait_layer, 0)

        def far_quarter(step, carry):
            r = lax.rem(y + 1 + step, NY)
            for g in range(4):
                qs = stacked(r, g)
                n = r * 4 + g
                s = []
                values = []
                for e in range(2):
                    b = choice[2 * g + e]
                    bias = jnp.where(b != c, 0.0, NEG).astype(jnp.float32)
                    s.append(scores(qs, kv[b, 0]) + bias)
                    values.append(kv[b, 1])
                m_own = own_max[n]
                m = jnp.maximum(
                    m_own, jnp.maximum(jnp.max(s[0], axis=1, keepdims=True), jnp.max(s[1], axis=1, keepdims=True))
                )
                scale = jnp.exp2((m_own - m) * EXP2)
                total = own_sum[n] * scale
                acc = own_acc[n] * scale
                for e in range(2):
                    p = jnp.exp2((s[e] - m) * EXP2)
                    total = total + jnp.sum(p, axis=1, keepdims=True)
                    acc = acc + jnp.dot(p.astype(jnp.bfloat16), values[e], preferred_element_type=jnp.float32)
                result = (acc / total).astype(jnp.bfloat16)
                for h in range(HEADS):
                    att_send[r, 32 * g:32 * g + 32, h * HD:(h + 1) * HD] = result[32 * h:32 * h + 32]

            @pl.when(r != y)
            def _():
                a_copy(r).start()

            @pl.when(r == y)
            def _():
                att_in[y] = att_send[r]
            return carry

        lax.fori_loop(0, NY, far_quarter, 0)

    def r_copy(n, way, stage, src, dst):
        return remote(src, dst, r_send.at[n, way, stage], r_recv.at[n, way, stage], up if way == 0 else down)

    def shard(step):
        return lax.rem(z + step, NZ)

    def stage_0(n):
        k, h = n // 2, lax.rem(n, 2)

        @pl.when((h == 0) & (k != y))
        def _():
            a_arrival(k).wait_recv()

        columns = pl.ds(pl.multiple_of(h * HALF, HALF), HALF)
        product = jnp.dot(att_in[k], w[:, columns], preferred_element_type=jnp.float32)
        part[n] = product.astype(jnp.bfloat16).reshape(NZ, 16, HALF)
        r_copy(n, 0, 0, part.at[n, shard(4), :, pl.ds(0, QUART)], rin0.at[n, 0]).start()
        r_copy(n, 1, 0, part.at[n, shard(4), :, pl.ds(QUART, QUART)], rin0.at[n, 1]).start()

    def stage_1(n):
        for way, step in ((0, 3), (1, 5)):
            d = shard(step)
            columns = pl.ds(way * QUART, QUART)
            r_copy(n, way, 0, rin0.at[n, way], rin0.at[n, way]).wait_recv()
            total = part[n, d, :, columns].astype(jnp.float32) + rin0[n, way].astype(jnp.float32)
            part[n, d, :, columns] = total.astype(jnp.bfloat16)
            r_copy(n, way, 1, part.at[n, d], rin.at[n, way, 0]).start()

    def stage_mid(n, stage):
        for way, step in ((0, 4 - stage), (1, 4 + stage)):
            d = shard(step)
            r_copy(n, way, stage - 1, rin.at[n, way, stage - 2], rin.at[n, way, stage - 2]).wait_recv()
            total = part[n, d].astype(jnp.float32) + rin[n, way, stage - 2].astype(jnp.float32)
            part[n, d] = total.astype(jnp.bfloat16)
            r_copy(n, way, stage, part.at[n, d], rin.at[n, way, stage - 1]).start()

    def f_copy(k, h):
        return remote(fin_send.at[k, h], fin_in.at[y, h], f_send.at[k, h], f_recv.at[y, h], row(k))

    def f_arrival(r, h):
        return remote(fin_in.at[r, h], fin_in.at[r, h], f_send.at[0, h], f_recv.at[r, h], row(lax.rem(y + 1, NY)))

    def stage_4(n):
        k, h = n // 2, lax.rem(n, 2)
        for way in range(2):
            r_copy(n, way, 3, rin.at[n, way, 2], rin.at[n, way, 2]).wait_recv()
        total = part[n, z].astype(jnp.float32) + rin[n, 0, 2].astype(jnp.float32) + rin[n, 1, 2].astype(jnp.float32)
        total = total.astype(jnp.bfloat16)

        @pl.when(k != y)
        def _():
            fin_send[k, h] = total
            f_copy(k, h).start()

        @pl.when(k == y)
        def _():
            fin_in[y, h] = total

    def tick(t):
        for stage, work in ((4, stage_4), (3, lambda n: stage_mid(n, 3)), (2, lambda n: stage_mid(n, 2)),
                            (1, stage_1), (0, stage_0)):
            n = t - stage

            @pl.when((n >= 0) & (n < CHUNKS))
            def _():
                work(n)

    gather(jnp.int32(1))
    w_copy.wait()

    def round_(step, carry):
        tick(step - 2)

        @pl.when(lax.rem(step, 2) == 0)
        def _():
            gather(step // 2 + 2)

            @pl.when(y == step // 2)
            def _():
                far_attention()
        return carry

    lax.fori_loop(0, CHUNKS + 4 + 2, round_, 0)

    for r in range(NY):
        for h in range(2):
            @pl.when(y != r)
            def _():
                f_arrival(r, h).wait_recv()
            rows, columns = pl.ds(16 * r, 16), pl.ds(h * HALF, HALF)
            total = res_ref[rows, columns].astype(jnp.float32) + fin_in[r, h].astype(jnp.float32)
            out_ref[rows, columns] = total.astype(jnp.bfloat16)

    for step in range(1, NY):
        @pl.when(y + step < NY)
        def _():
            y_copy(step).wait_send()

    def drain_layer(j, carry):
        for n in range(8):
            x_send_copy(j, n).wait_send()
        return carry

    lax.fori_loop(0, y + 1, drain_layer, 0)
    for r in range(NY):
        @pl.when(y != r)
        def _():
            a_copy(r).wait_send()
            for h in range(2):
                f_copy(r, h).wait_send()

    def drain_chunk(n, carry):
        for way in range(2):
            r_copy(n, way, 0, rin0.at[n, way], rin0.at[n, way]).wait_send()
            for stage in (1, 2, 3):
                r_copy(n, way, stage, rin.at[n, way, stage - 1], rin.at[n, way, stage - 1]).wait_send()
        return carry

    lax.fori_loop(0, CHUNKS, drain_chunk, 0)


def body(query_rows, key_rows, value_rows, block_choice, out_weight, residual):
    choice = block_choice[0, 0, ::BLK // 4, 0, 1:].reshape(8)
    q = query_rows.reshape(BLK, HEADS * HD)
    k = key_rows.reshape(BLK, HD)
    v = value_rows.reshape(BLK, HD)
    res = residual.reshape(BLK // NZ, WIDTH)
    vmem = pl.BlockSpec(memory_space=pltpu.VMEM)
    bf16, f32 = jnp.bfloat16, jnp.float32
    dma = pltpu.SemaphoreType.DMA
    out = pl.pallas_call(
        kernel,
        out_shape=jax.ShapeDtypeStruct((BLK // NZ, WIDTH), bf16),
        in_specs=[pl.BlockSpec(memory_space=pltpu.SMEM), vmem, vmem, vmem, pl.BlockSpec(memory_space=pl.ANY), vmem],
        out_specs=vmem,
        scratch_shapes=[
            pltpu.VMEM((2 * NX * NY, 2, BLK, HD), bf16),
            pltpu.VMEM((HEADS * HD, WIDTH), bf16),
            pltpu.VMEM((16, 128, HD), f32),
            pltpu.VMEM((16, 128, 1), f32),
            pltpu.VMEM((16, 128, 1), f32),
            pltpu.VMEM((NY, 128, HEADS * HD), bf16),
            pltpu.VMEM((NY, 128, HEADS * HD), bf16),
            pltpu.VMEM((CHUNKS, NZ, 16, HALF), bf16),
            pltpu.VMEM((CHUNKS, 2, 16, QUART), bf16),
            pltpu.VMEM((CHUNKS, 2, 3, 16, HALF), bf16),
            pltpu.VMEM((NY, 2, 16, HALF), bf16),
            pltpu.VMEM((NY, 2, 16, HALF), bf16),
            dma, dma((NY - 1,)), dma((NY,)), dma((NY, 8)), dma((NY, 8)), dma((NY,)), dma((NY,)),
            dma((CHUNKS, 2, 4)), dma((CHUNKS, 2, 4)), dma((NY, 2)), dma((NY, 2)),
        ],
        compiler_params=pltpu.CompilerParams(
            collective_id=1, has_side_effects=True, vmem_limit_bytes=48 * 1024 * 1024
        ),
        name="attention_mix",
    )(choice, q, k, v, out_weight, res)
    return out.reshape(1, 1, BLK // NZ, WIDTH)


def solution(mesh):
    placed = (
        P(None, "ctx", None, "tp"),
        P(None, "ctx", None, "tp"),
        P(None, "ctx", None, "tp"),
        P(None, "ctx", None, "tp", None),
        P("tp", None),
        P(None, "ctx", "tp", None),
    )
    return jax.shard_map(
        body, mesh=mesh, in_specs=placed, out_specs=P(None, "ctx", "tp", None), check_vma=False
    )
```

time: 382 us -> 103 us (0.27)
  waiting for transfers between devices: 195 us -> 0 us
  Pallas kernels: 0 us -> 94.7 us
  local copies, waits for them, and re-layouts: 64 us -> 7.83 us
  matrix products: 39 us -> 0 us
  other arithmetic: 32.8 us -> 0 us
  starting transfers between devices: 21.5 us -> 0 us
  between operations: 13.7 us -> 0.02 us
  blocking collectives: 12.8 us -> 0 us
    all_to_all x3 -> x0, waiting for transfers between devices: 137 us -> none  [the longest x1 91.5 us: body(): lax.all_to_all(pooled_all, 'ctx', split_axis=0, concat_axis=0, tiled=True)]
    pallas_call x0 -> x1, Pallas kernels: none -> 94.7 us  [body(): pl.pallas_call(kernel, out_shape=jax.ShapeDtypeStruct((BLK // NZ, WIDTH),...]
    reduce_scatter x1 -> x0, waiting for transfers between devices: 58.1 us -> none  [body(): lax.psum_scatter(jnp.dot(rows_now, out_weight, preferred_element_type=jnp...]
    dot_general x19 -> x0, matrix products: 39 us -> none  [the longest x9 17.6 us: soft_pool(): jnp.einsum(pattern, weights.astype(jnp.bfloat16), value_block, preferred_...]
    all_to_all x3 -> x0, starting transfers between devices: 21.3 us -> none  [the longest x1 7.41 us: body(): lax.all_to_all(row_send, 'ctx', split_axis=0, concat_axis=0, tiled=True)]
    reshape x2 -> x0, local copies, waits for them, and re-layouts: 18.9 us -> none  [body(): flat_pooled = pooled_back.reshape(slot_total, group_size, HD)[clipped]]
    reduce_sum x12 -> x0, other arithmetic: 17 us -> none  [the longest x9 12.6 us: soft_pool(): total = jnp.sum(weights, axis=-1, keepdims=True)]
    all_to_all x1 -> x0, blocking collectives: 12.8 us -> none  [body(): lax.all_to_all(logsum_all, 'ctx', split_axis=0, concat_axis=0, tiled=True)]
  transfers between devices with their start and end apart: 4 -> 0, of which waited for: 3 -> 0; matrix products, arithmetic and copies ran while one was open for 5% -> 0% of each run, Pallas kernels for 0% -> 0%
where the time goes in v1:
time: 103 us
  Pallas kernels  94.7 us (92%)
  local copies, waits for them, and re-layouts  7.83 us (8%)
    pallas_call x1, Pallas kernels, body(): pl.pallas_call(kernel, out_shape=jax.ShapeDtypeStruct((BLK // NZ, WIDTH),...  94.7 us
    unnamed x11, local copies, waits for them, and re-layouts  6.87 us

profile of v1, /device:TPU:24, one launch (start us, length us, event | category | flops | bytes accessed | tf_op | source)
XLA Modules:
  0.0 102.6 jit_solution(10630787227790919913)
XLA Ops:
  0.0 0.8 slice.3
  0.8 0.1 copy.8
  0.9 0.1 reshape_squeeze.3.choice
  1.0 0.0 copy-start
  1.0 2.2 %copy-done = bf16[512,4096]{1,0:T(8,128)(2,1)S(1)} copy-done((bf16[512,4096]{1,0:T(8,128)(2,1)S(1)}, bf16[512,4096]{1,0:T(8,128)(2,1)}, u32[]{:S(2)}) %copy-start) | copy-done | bytes 4194328
  3.1 0.0 copy-start.1
  3.1 1.0 %copy-done.1 = bf16[1,1,512,512]{3,2,1,0:T(8,128)(2,1)S(1)} copy-done((bf16[1,1,512,512]{3,2,1,0:T(8,128)(2,1)S(1)}, bf16[1,1,512,512]{3,2,1,0:T(8,128)(2,1)}, u32[]{:S(2)}) %copy-start.1) | copy-done | bytes 524312
  4.2 0.0 copy-start.2
  4.2 1.0 %copy-done.2 = bf16[1,1,64,4096]{3,2,1,0:T(8,128)(2,1)S(1)} copy-done((bf16[1,1,64,4096]{3,2,1,0:T(8,128)(2,1)S(1)}, bf16[1,1,64,4096]{3,2,1,0:T(8,128)(2,1)}, u32[]{:S(2)}) %copy-start.2) | copy-done | bytes 524312
  5.2 0.0 copy-start.3
  5.2 0.9 copy-done.3
  6.1 0.0 copy-start.4
  6.1 0.9 copy-done.4
  7.0 94.7 %attention_mix.1 = bf16[64,4096]{1,0:T(8,128)(2,1)S(1)} custom-call(s32[8]{0:T(128)S(1)} %reshape_squeeze.3.choice, bf16[512,512]{1,0:T(8,128)(2,1)S(1)} %bitcast.8, bf16[512,128]{1,0:T(8,128)(2,1)S(1)} %bitcast.10, bf16[512,128]{1,0:T(8,128)(2,1)S(1)} %bitcast.11, bf16[512,4096]{1,0:T(8,128)(2,1)S(1)} %copy-done, bf16[64,4096]{1,0:T(8,128)(2,1)S(1)} %bitcast.9), custom_call_target="tpu_custom_call" | custom-call | tf_op jit(solution)/shard_map/attention_mix/pallas_call | solution.py:341
  101.8 0.8 copy.10
Async XLA Ops:
  1.0 2.2 %copy-start = (bf16[512,4096]{1,0:T(8,128)(2,1)S(1)}, bf16[512,4096]{1,0:T(8,128)(2,1)}, u32[]{:S(2)}) copy-start(bf16[512,4096]{1,0:T(8,128)(2,1)} %w_hbm.1) | copy-start | bytes 12582916
  3.1 1.0 %copy-start.1 = (bf16[1,1,512,512]{3,2,1,0:T(8,128)(2,1)S(1)}, bf16[1,1,512,512]{3,2,1,0:T(8,128)(2,1)}, u32[]{:S(2)}) copy-start(bf16[1,1,512,512]{3,2,1,0:T(8,128)(2,1)} %param.6) | copy-start | bytes 1572868
  4.2 1.0 %copy-start.2 = (bf16[1,1,64,4096]{3,2,1,0:T(8,128)(2,1)S(1)}, bf16[1,1,64,4096]{3,2,1,0:T(8,128)(2,1)}, u32[]{:S(2)}) copy-start(bf16[1,1,64,4096]{3,2,1,0:T(8,128)(2,1)} %param.11) | copy-start | bytes 1572868
  5.2 0.9 copy-start.3
  6.1 0.9 copy-start.4

commit v2 on v1

v2 whole, which is shorter than its diff:
```python
import functools
import math

import jax
import jax.numpy as jnp
from jax import lax
from jax.experimental import pallas as pl
from jax.experimental.pallas import tpu as pltpu
from jax.sharding import PartitionSpec as P

MESH = pl.DeviceIdType.MESH
HD = 128
HEADS = 4
BLK = 512
NX, NY, NZ = 4, 4, 8
WIDTH = 4096
CHUNKS = 8
PER_ROW = CHUNKS // NY
HALF = WIDTH // PER_ROW
QUART = HALF // 2
SKEW = 1
NEG = -1e30
SHARE_AT = ((2, 1), (3, 2))
FAR_AT = (-1, -1, 2, 4)
EXP2 = math.log2(math.e) / math.sqrt(HD)


def kernel(
    choice_hbm, q_hbm, k_hbm, v_hbm, w_hbm, res_hbm, out_ref,
    choice, q_ref, res_ref, kv, w, own_acc, own_max, own_sum, att_send, att_in, part, rin0, rin, fin_send, fin_in,
    in_sem, y_send, y_recv, x_send, x_recv, a_send, a_recv, r_send, r_recv, f_send, f_recv,
):
    c = lax.axis_index("ctx")
    z = lax.axis_index("tp")
    core = lax.rem(c, 2)
    x = lax.rem(c // 2, NX)
    y = c // (2 * NX)

    def index(xx, yy, cc):
        return (yy * NX + xx) * 2 + cc

    x_next, x_prev = lax.rem(x + 1, NX), lax.rem(x + NX - 1, NX)
    x_far = lax.rem(x + 2, NX)
    right = (index(x_next, y, core), z)
    left = (index(x_prev, y, core), z)
    sibling = (index(x, y, 1 - core), z)
    up = (c, lax.rem(z + 1, NZ))
    down = (c, lax.rem(z + NZ - 1, NZ))

    def row(yy):
        return (index(x, yy, core), z)

    def remote(src, dst, s_sem, r_sem, device):
        return pltpu.make_async_remote_copy(
            src_ref=src, dst_ref=dst, send_sem=s_sem, recv_sem=r_sem, device_id=device, device_id_type=MESH
        )

    barrier = pltpu.get_barrier_semaphore()
    for device in (right, left, sibling, up, down):
        pl.semaphore_signal(barrier, inc=1, device_id=device, device_id_type=MESH)
    for step in range(1, NY):
        pl.semaphore_signal(barrier, inc=1, device_id=row(lax.rem(y + step, NY)), device_id_type=MESH)
    k_copy, v_copy, q_copy, w_copy, choice_copy, res_copy = [
        pltpu.make_async_copy(src, dst, in_sem.at[n])
        for n, (src, dst) in enumerate(
            [(k_hbm, kv.at[c, 0]), (v_hbm, kv.at[c, 1]), (q_hbm, q_ref), (w_hbm, w), (choice_hbm, choice),
             (res_hbm, res_ref)]
        )
    ]
    for copy in (k_copy, v_copy, q_copy, choice_copy):
        copy.start()
    pl.semaphore_wait(barrier, 8)

    def y_copy(far, n, layer, target):
        b = index(x_far if far else x, layer, core)
        return remote(kv.at[b], kv.at[b], y_send.at[far, n], y_recv.at[far, layer], row(target))

    def y_own(far, n):
        return y_copy(far, n, y, lax.rem(y + 1, NY) if n == 0 else NY - 1)

    def y_relay(far):
        return y_copy(far, 2, lax.rem(NY + 3 - y, NY), lax.rem(NY + 5 - y, NY))

    def y_wait(far, layer):
        y_copy(far, 0, layer, lax.rem(y + 1, NY)).wait_recv()

    def y_start(far):
        @pl.when(y < NY - 1)
        def _():
            y_own(far, 0).start()

        @pl.when(y == 0)
        def _():
            y_own(far, 1).start()

    def y_pass_on(far):
        @pl.when(y == 3)
        def _():
            y_wait(far, 0)

        @pl.when(y >= 2)
        def _():
            y_relay(far).start()

    def blocks(j, cc):
        layer = y - j
        return [index(xx, layer, cc) for xx in (x, x_prev, x_next, x_far)]

    def x_copy(j, n, src, device):
        return remote(src, src, x_send.at[j, n], x_recv.at[j, n], device)

    def x_send_copy(j, n):
        mine, prev, nxt, far = blocks(j, core)
        if n < 4 and j == 0:
            src, half = (k_hbm, 0) if n in (0, 3) else (v_hbm, 1)
            device = right if n in (0, 2) else left
            return remote(src, kv.at[mine, half], x_send.at[0, n], x_recv.at[0, n], device)
        src, device = [
            (kv.at[mine], right), (kv.at[mine], left), None, None,
            (kv.at[prev, 0], right), (kv.at[nxt, 1], left),
            (kv.at[mine], sibling), (kv.at[prev], sibling), (kv.at[nxt], sibling), (kv.at[far], sibling),
        ][n]
        return x_copy(j, n, src, device)

    def x_arrival(j, n):
        mine, prev, nxt, far = blocks(j, core)
        ref = [kv.at[prev, 0], kv.at[nxt, 1], kv.at[prev, 1], kv.at[nxt, 0], kv.at[far, 0], kv.at[far, 1]][n]
        return x_copy(j, n, ref, sibling)

    def x_block_arrival(j, n):
        _, prev, nxt, _ = blocks(j, core)
        return x_copy(j, n, kv.at[(prev, nxt)[n]], sibling)

    def sibling_arrival(j, n):
        return x_copy(j, 6 + n, kv.at[blocks(j, 1 - core)[n]], sibling)

    def gather_start(j):
        @pl.when(j <= y)
        def _():
            x_send_copy(j, 0).start()
            x_send_copy(j, 1).start()
            if j == 0:
                x_send_copy(j, 2).start()
                x_send_copy(j, 3).start()
                w_copy.start()
                res_copy.start()
                k_copy.wait()
                v_copy.wait()
            x_send_copy(j, 6).start()

    def gather_forward():
        x_arrival(0, 0).wait_recv()
        x_send_copy(0, 4).start()
        x_arrival(0, 1).wait_recv()
        x_send_copy(0, 5).start()

    def gather_share(j):
        @pl.when(j <= y)
        def _():
            if j == 0:
                x_arrival(j, 2).wait_recv()
            else:
                x_block_arrival(j, 0).wait_recv()
            x_send_copy(j, 7).start()
            if j == 0:
                x_arrival(j, 3).wait_recv()
            else:
                x_block_arrival(j, 1).wait_recv()
            x_send_copy(j, 8).start()
            if j == 0:
                x_arrival(j, 4).wait_recv()
                x_arrival(j, 5).wait_recv()
            elif j < 3:
                y_wait(1, y - j)
            x_send_copy(j, 9).start()

    gather_start(0)
    y_start(0)

    def stacked(quarters, g):
        rows = []
        for r in quarters:
            for h in range(HEADS):
                for u in (2 * g, 2 * g + 1):
                    start = pl.multiple_of(64 * u + 16 * r, 16)
                    rows.append(q_ref[pl.ds(start, 16), h * HD:(h + 1) * HD])
        return jnp.concatenate(rows, axis=0)

    def scores(qs, keys):
        return lax.dot_general(qs, keys, (((1,), (1,)), ((), ())), preferred_element_type=jnp.float32)

    def own_attention():
        a = lax.broadcasted_iota(jnp.int32, (4 * 128, 128), 0)
        token = 64 * (lax.rem(a, 32) // 16) + 16 * (a // 128) + lax.rem(a, 16)
        key = lax.broadcasted_iota(jnp.int32, (4 * 128, 128), 1)
        for g in range(4):
            qs = stacked(range(4), g)
            last, before = pl.ds(128 * g, 128), pl.ds(0, 128 * g)
            s = jnp.where(key <= token, scores(qs, kv[c, 0, last]), NEG)
            m = jnp.max(s, axis=1, keepdims=True)
            if g > 0:
                s_before = scores(qs, kv[c, 0, before])
                m = jnp.maximum(m, jnp.max(s_before, axis=1, keepdims=True))
            p = jnp.exp2((s - m) * EXP2)
            total = jnp.sum(p, axis=1, keepdims=True)
            acc = jnp.dot(p.astype(jnp.bfloat16), kv[c, 1, last], preferred_element_type=jnp.float32)
            if g > 0:
                p = jnp.exp2((s_before - m) * EXP2)
                total = total + jnp.sum(p, axis=1, keepdims=True)
                acc = acc + jnp.dot(p.astype(jnp.bfloat16), kv[c, 1, before], preferred_element_type=jnp.float32)
            own_max[g] = m
            own_sum[g] = total
            own_acc[g] = acc

    q_copy.wait()
    own_attention()

    def a_copy(r):
        return remote(att_send.at[r], att_in.at[y], a_send.at[r], a_recv.at[y], row(r))

    def a_arrival(k):
        return remote(att_in.at[k], att_in.at[k], a_send.at[0], a_recv.at[k], row(lax.rem(y + 1, NY)))

    def far_attention():
        def wait_layer(j, carry):
            for n in range(4):
                sibling_arrival(j, n).wait_recv()
            return carry

        lax.fori_loop(0, y + 1, wait_layer, 0)

        def far_pair(step, carry):
            pair = lax.rem(y // 2 + 1 + step, 2)
            quarters = [2 * pair, 2 * pair + 1]
            rows = pl.ds(pl.multiple_of(256 * pair, 256), 256)

            for g in range(4):
                qs = stacked(quarters, g)
                s, tops, biases, values = [], [], [], []
                for e in range(2):
                    b = choice[1 + e, 0, 128 * g]
                    bias = jnp.where(b != c, 0.0, NEG).astype(jnp.float32)
                    s.append(scores(qs, kv[b, 0]))
                    tops.append(jnp.max(s[e], axis=1, keepdims=True) + bias)
                    biases.append(bias)
                    values.append(kv[b, 1])
                m_own = own_max[g, rows]
                m = jnp.maximum(m_own, jnp.maximum(tops[0], tops[1]))
                scale = jnp.exp2((m_own - m) * EXP2)
                total = own_sum[g, rows] * scale
                acc = own_acc[g, rows] * scale
                for e in range(2):
                    p = jnp.exp2((s[e] - (m - biases[e])) * EXP2)
                    total = total + jnp.sum(p, axis=1, keepdims=True)
                    acc = acc + jnp.dot(p.astype(jnp.bfloat16), values[e], preferred_element_type=jnp.float32)
                result = (acc / total).astype(jnp.bfloat16)
                to = pl.ds(32 * g, 32)
                for n, r in enumerate(quarters):
                    for h in range(HEADS):
                        first = 128 * n + 32 * h
                        att_send[r, to, h * HD:(h + 1) * HD] = result[first:first + 32]
            for r in quarters:
                @pl.when(r != y)
                def _():
                    a_copy(r).start()

                @pl.when(r == y)
                def _():
                    att_in[y] = att_send[r]
            return carry

        lax.fori_loop(0, 2, far_pair, 0)

    def r_copy(n, way, stage, src, dst):
        return remote(src, dst, r_send.at[n, way, stage], r_recv.at[n, way, stage], up if way == 0 else down)

    def shard(step):
        return lax.rem(z + step, NZ)

    def stage_0(n):
        k, h = n // PER_ROW, lax.rem(n, PER_ROW)

        @pl.when((h == 0) & (k != y))
        def _():
            a_arrival(k).wait_recv()

        columns = pl.ds(pl.multiple_of(h * HALF, HALF), HALF)
        product = jnp.dot(att_in[k], w[:, columns], preferred_element_type=jnp.float32)
        part[n] = product.astype(jnp.bfloat16).reshape(NZ, 16, HALF)
        r_copy(n, 0, 0, part.at[n, shard(4), :, pl.ds(0, QUART)], rin0.at[n, 0]).start()
        r_copy(n, 1, 0, part.at[n, shard(4), :, pl.ds(QUART, QUART)], rin0.at[n, 1]).start()

    def stage_1(n):
        for way, step in ((0, 3), (1, 5)):
            d = shard(step)
            columns = pl.ds(way * QUART, QUART)
            r_copy(n, way, 0, rin0.at[n, way], rin0.at[n, way]).wait_recv()
            total = part[n, d, :, columns].astype(jnp.float32) + rin0[n, way].astype(jnp.float32)
            part[n, d, :, columns] = total.astype(jnp.bfloat16)
            r_copy(n, way, 1, part.at[n, d], rin.at[n, way, 0]).start()

    def stage_mid(n, stage):
        for way, step in ((0, 4 - stage), (1, 4 + stage)):
            d = shard(step)
            r_copy(n, way, stage - 1, rin.at[n, way, stage - 2], rin.at[n, way, stage - 2]).wait_recv()
            total = part[n, d].astype(jnp.float32) + rin[n, way, stage - 2].astype(jnp.float32)
            part[n, d] = total.astype(jnp.bfloat16)
            r_copy(n, way, stage, part.at[n, d], rin.at[n, way, stage - 1]).start()

    def f_copy(k, h):
        return remote(fin_send.at[k, h], fin_in.at[y, h], f_send.at[k, h], f_recv.at[y, h], row(k))

    def f_arrival(r, h):
        return remote(fin_in.at[r, h], fin_in.at[r, h], f_send.at[0, h], f_recv.at[r, h], row(lax.rem(y + 1, NY)))

    def stage_4(n):
        k, h = n // PER_ROW, lax.rem(n, PER_ROW)
        for way in range(2):
            r_copy(n, way, 3, rin.at[n, way, 2], rin.at[n, way, 2]).wait_recv()
        total = part[n, z].astype(jnp.float32) + rin[n, 0, 2].astype(jnp.float32) + rin[n, 1, 2].astype(jnp.float32)
        total = total.astype(jnp.bfloat16)

        @pl.when(k != y)
        def _():
            fin_send[k, h] = total
            f_copy(k, h).start()

        @pl.when(k == y)
        def _():
            fin_in[y, h] = total

    def tick(t):
        for stage, work in ((0, stage_0), (1, stage_1), (2, lambda n: stage_mid(n, 2)),
                            (3, lambda n: stage_mid(n, 3)), (4, stage_4)):
            n = t - SKEW * stage

            @pl.when((n >= 0) & (n < CHUNKS))
            def _():
                work(n)

    gather_forward()

    @pl.when(y >= 1)
    def _():
        y_wait(0, y - 1)
    y_pass_on(0)
    gather_start(1)
    w_copy.wait()
    choice_copy.wait()
    res_copy.wait()

    def round_(step, carry):
        t = step - 1
        tick(t)

        @pl.when(t == -1)
        def _():
            gather_share(0)
            y_start(1)

            @pl.when(y >= 2)
            def _():
                y_wait(0, y - 2)
            gather_start(2)
            gather_start(3)
            gather_share(1)
            y_pass_on(1)

        for j, at in SHARE_AT:
            @pl.when(t == at)
            def _():
                gather_share(j)

        far_at = sum(jnp.where(y == j, at, 0) for j, at in enumerate(FAR_AT))

        @pl.when(t == far_at)
        def _():
            far_attention()
        return carry

    lax.fori_loop(0, CHUNKS + 4 * SKEW + 1, round_, 0)

    for r in range(NY):
        for h in range(PER_ROW):
            @pl.when(y != r)
            def _():
                f_arrival(r, h).wait_recv()
            rows, columns = pl.ds(16 * r, 16), pl.ds(h * HALF, HALF)
            total = res_ref[rows, columns].astype(jnp.float32) + fin_in[r, h].astype(jnp.float32)
            out_ref[rows, columns] = total.astype(jnp.bfloat16)

    for far in range(2):
        @pl.when(y < NY - 1)
        def _():
            y_own(far, 0).wait_send()

        @pl.when(y == 0)
        def _():
            y_own(far, 1).wait_send()

        @pl.when(y >= 2)
        def _():
            y_relay(far).wait_send()
    for j in range(NY):
        @pl.when(j <= y)
        def _():
            for n in range(10) if j == 0 else (0, 1, 6, 7, 8, 9):
                x_send_copy(j, n).wait_send()
    for r in range(NY):
        @pl.when(y != r)
        def _():
            a_copy(r).wait_send()
            for h in range(PER_ROW):
                f_copy(r, h).wait_send()

    def drain_chunk(n, carry):
        for way in range(2):
            r_copy(n, way, 0, rin0.at[n, way], rin0.at[n, way]).wait_send()
            for stage in (1, 2, 3):
                r_copy(n, way, stage, rin.at[n, way, stage - 1], rin.at[n, way, stage - 1]).wait_send()
        return carry

    lax.fori_loop(0, CHUNKS, drain_chunk, 0)


def body(query_rows, key_rows, value_rows, block_choice, out_weight, residual):
    choice = jnp.transpose(block_choice, (0, 1, 4, 3, 2)).reshape(3, 1, BLK)
    q = query_rows.reshape(BLK, HEADS * HD)
    k = key_rows.reshape(BLK, HD)
    v = value_rows.reshape(BLK, HD)
    res = residual.reshape(BLK // NZ, WIDTH)
    vmem, hbm = pl.BlockSpec(memory_space=pltpu.VMEM), pl.BlockSpec(memory_space=pl.ANY)
    bf16, f32 = jnp.bfloat16, jnp.float32
    dma = pltpu.SemaphoreType.DMA
    out = pl.pallas_call(
        kernel,
        out_shape=jax.ShapeDtypeStruct((BLK // NZ, WIDTH), bf16),
        in_specs=[hbm] * 6,
        out_specs=vmem,
        scratch_shapes=[
            pltpu.SMEM((3, 1, BLK), jnp.int32),
            pltpu.VMEM((BLK, HEADS * HD), bf16),
            pltpu.VMEM((BLK // NZ, WIDTH), bf16),
            pltpu.VMEM((2 * NX * NY, 2, BLK, HD), bf16),
            pltpu.VMEM((HEADS * HD, WIDTH), bf16),
            pltpu.VMEM((4, BLK, HD), f32),
            pltpu.VMEM((4, BLK, 1), f32),
            pltpu.VMEM((4, BLK, 1), f32),
            pltpu.VMEM((NY, 128, HEADS * HD), bf16),
            pltpu.VMEM((NY, 128, HEADS * HD), bf16),
            pltpu.VMEM((CHUNKS, NZ, 16, HALF), bf16),
            pltpu.VMEM((CHUNKS, 2, 16, QUART), bf16),
            pltpu.VMEM((CHUNKS, 2, 3, 16, HALF), bf16),
            pltpu.VMEM((NY, PER_ROW, 16, HALF), bf16),
            pltpu.VMEM((NY, PER_ROW, 16, HALF), bf16),
            dma((6,)), dma((2, 3)), dma((2, NY)), dma((NY, 10)), dma((NY, 10)), dma((NY,)), dma((NY,)),
            dma((CHUNKS, 2, 4)), dma((CHUNKS, 2, 4)), dma((NY, PER_ROW)), dma((NY, PER_ROW)),
        ],
        compiler_params=pltpu.CompilerParams(
            collective_id=1, has_side_effects=True, vmem_limit_bytes=62 * 1024 * 1024
        ),
        name="attention_mix",
    )(choice, q, k, v, out_weight, res)
    return out.reshape(1, 1, BLK // NZ, WIDTH)


def solution(mesh):
    placed = (
        P(None, "ctx", None, "tp"),
        P(None, "ctx", None, "tp"),
        P(None, "ctx", None, "tp"),
        P(None, "ctx", None, "tp", None),
        P("tp", None),
        P(None, "ctx", "tp", None),
    )
    return jax.shard_map(
        body, mesh=mesh, in_specs=placed, out_specs=P(None, "ctx", "tp", None), check_vma=False
    )
```

time: 103 us -> 86.3 us (0.84)
  Pallas kernels: 94.7 us -> 84.3 us
  local copies, waits for them, and re-layouts: 7.83 us -> 1.87 us
    pallas_call x1, Pallas kernels: 94.7 us -> 84.3 us  [body(): pl.pallas_call(kernel, out_shape=jax.ShapeDtypeStruct((BLK // NZ, WIDTH),...]
    unnamed x11 -> x1, local copies, waits for them, and re-layouts: 6.87 us -> 1.87 us
where the time goes in v2:
time: 86.3 us; the launch traced here: 86.1 us
  Pallas kernels  84.3 us (98%)
  local copies, waits for them, and re-layouts  1.87 us (2%)
    pallas_call x1, Pallas kernels, body(): pl.pallas_call(kernel, out_shape=jax.ShapeDtypeStruct((BLK // NZ, WIDTH),...  84.3 us
    unnamed x1, local copies, waits for them, and re-layouts  1.87 us

profile of v2, /device:TPU:24, one launch (start us, length us, event | category | flops | bytes accessed | tf_op | source)
XLA Modules:
  0.0 86.1 jit_solution(17036357810334003048)
XLA Ops:
  0.0 84.3 %attention_mix.1 = bf16[64,4096]{1,0:T(8,128)(2,1)} custom-call(s32[3,1,512]{2,1,0:T(1,128)} %bitcast.13, bf16[512,512]{1,0:T(8,128)(2,1)} %bitcast.9, bf16[512,128]{1,0:T(8,128)(2,1)} %bitcast.11, bf16[512,128]{1,0:T(8,128)(2,1)} %bitcast.12, bf16[512,4096]{1,0:T(8,128)(2,1)} %w_hbm.1, bf16[64,4096]{1,0:T(8,128)(2,1)} %bitcast.10), custom_call_target="tpu_custom_call" | custom-call | tf_op jit(solution)/shard_map/attention_mix/pallas_call | solution.py:435
  84.3 1.9 %copy.8 = bf16[1,1,64,4096]{3,2,1,0:T(8,128)(2,1)} copy(bf16[1,1,64,4096]{3,2,1,0:T(8,128)(2,1)} %bitcast.8) | data formatting | bytes 1048576

commit v3 on v2

--- a/solution.py
+++ b/solution.py
@@ -27,7 +27,7 @@
 
 def kernel(
     choice_hbm, q_hbm, k_hbm, v_hbm, w_hbm, res_hbm, out_ref,
-    choice, q_ref, res_ref, kv, w, own_acc, own_max, own_sum, att_send, att_in, part, rin0, rin, fin_send, fin_in,
+    choice, q_ref, v_ref, res_ref, kv, w, own_acc, own_max, own_sum, att_send, att_in, part, rin0, rin, fin_send, fin_in,
     in_sem, y_send, y_recv, x_send, x_recv, a_send, a_recv, r_send, r_recv, f_send, f_recv,
 ):
     c = lax.axis_index("ctx")
@@ -63,7 +63,7 @@
     k_copy, v_copy, q_copy, w_copy, choice_copy, res_copy = [
         pltpu.make_async_copy(src, dst, in_sem.at[n])
         for n, (src, dst) in enumerate(
-            [(k_hbm, kv.at[c, 0]), (v_hbm, kv.at[c, 1]), (q_hbm, q_ref), (w_hbm, w), (choice_hbm, choice),
+            [(k_hbm, kv.at[c, 0]), (v_hbm, v_ref), (q_hbm, q_ref), (w_hbm, w), (choice_hbm, choice),
              (res_hbm, res_ref)]
         )
     ]
@@ -112,7 +112,7 @@
     def x_send_copy(j, n):
         mine, prev, nxt, far = blocks(j, core)
         if n < 4 and j == 0:
-            src, half = (k_hbm, 0) if n in (0, 3) else (v_hbm, 1)
+            src, half = (k_hbm, 0) if n in (0, 3) else (kv.at[mine, 1], 1)
             device = right if n in (0, 2) else left
             return remote(src, kv.at[mine, half], x_send.at[0, n], x_recv.at[0, n], device)
         src, device = [
@@ -138,14 +138,18 @@
         @pl.when(j <= y)
         def _():
             x_send_copy(j, 0).start()
+            if j == 0:
+                x_send_copy(j, 3).start()
+                v_copy.wait()
+                for n in range(4):
+                    part_rows = pl.ds(HD * n, HD)
+                    kv[c, 1, part_rows] = v_ref[part_rows, :].T
             x_send_copy(j, 1).start()
             if j == 0:
                 x_send_copy(j, 2).start()
-                x_send_copy(j, 3).start()
+                k_copy.wait()
                 w_copy.start()
                 res_copy.start()
-                k_copy.wait()
-                v_copy.wait()
             x_send_copy(j, 6).start()
 
     def gather_forward():
@@ -189,25 +193,28 @@
     def scores(qs, keys):
         return lax.dot_general(qs, keys, (((1,), (1,)), ((), ())), preferred_element_type=jnp.float32)
 
+    def values(b, first, last):
+        return jnp.concatenate([kv[b, 1, HD * n:HD * (n + 1)] for n in range(first, last)], axis=1)
+
     def own_attention():
-        a = lax.broadcasted_iota(jnp.int32, (4 * 128, 128), 0)
+        a = lax.broadcasted_iota(jnp.int32, (128, BLK), 1)
         token = 64 * (lax.rem(a, 32) // 16) + 16 * (a // 128) + lax.rem(a, 16)
-        key = lax.broadcasted_iota(jnp.int32, (4 * 128, 128), 1)
+        key = lax.broadcasted_iota(jnp.int32, (128, BLK), 0)
         for g in range(4):
             qs = stacked(range(4), g)
             last, before = pl.ds(128 * g, 128), pl.ds(0, 128 * g)
-            s = jnp.where(key <= token, scores(qs, kv[c, 0, last]), NEG)
-            m = jnp.max(s, axis=1, keepdims=True)
+            s = jnp.where(key <= token, scores(kv[c, 0, last], qs), NEG)
+            m = jnp.max(s, axis=0, keepdims=True)
             if g > 0:
-                s_before = scores(qs, kv[c, 0, before])
-                m = jnp.maximum(m, jnp.max(s_before, axis=1, keepdims=True))
+                s_before = scores(kv[c, 0, before], qs)
+                m = jnp.maximum(m, jnp.max(s_before, axis=0, keepdims=True))
             p = jnp.exp2((s - m) * EXP2)
-            total = jnp.sum(p, axis=1, keepdims=True)
-            acc = jnp.dot(p.astype(jnp.bfloat16), kv[c, 1, last], preferred_element_type=jnp.float32)
+            total = jnp.sum(p, axis=0, keepdims=True)
+            acc = jnp.dot(values(c, g, g + 1), p.astype(jnp.bfloat16), preferred_element_type=jnp.float32)
             if g > 0:
                 p = jnp.exp2((s_before - m) * EXP2)
-                total = total + jnp.sum(p, axis=1, keepdims=True)
-                acc = acc + jnp.dot(p.astype(jnp.bfloat16), kv[c, 1, before], preferred_element_type=jnp.float32)
+                total = total + jnp.sum(p, axis=0, keepdims=True)
+                acc = acc + jnp.dot(values(c, 0, g), p.astype(jnp.bfloat16), preferred_element_type=jnp.float32)
             own_max[g] = m
             own_sum[g] = total
             own_acc[g] = acc
@@ -234,26 +241,31 @@
             quarters = [2 * pair, 2 * pair + 1]
             rows = pl.ds(pl.multiple_of(256 * pair, 256), 256)
 
+            def group_scores(g):
+                qs = stacked(quarters, g)
+                return [scores(kv[choice[1 + e, 0, 128 * g], 0], qs) for e in range(2)]
+
+            later = group_scores(0)
             for g in range(4):
-                qs = stacked(quarters, g)
-                s, tops, biases, values = [], [], [], []
+                s = later
+                if g < 3:
+                    later = group_scores(g + 1)
+                chosen = [choice[1 + e, 0, 128 * g] for e in range(2)]
+                bias = [jnp.where(b != c, 0.0, NEG).astype(jnp.float32) for b in chosen]
+                m_own = own_max[g, :, rows]
+                m = m_own
                 for e in range(2):
-                    b = choice[1 + e, 0, 128 * g]
-                    bias = jnp.where(b != c, 0.0, NEG).astype(jnp.float32)
-                    s.append(scores(qs, kv[b, 0]))
-                    tops.append(jnp.max(s[e], axis=1, keepdims=True) + bias)
-                    biases.append(bias)
-                    values.append(kv[b, 1])
-                m_own = own_max[g, rows]
-                m = jnp.maximum(m_own, jnp.maximum(tops[0], tops[1]))
+                    m = jnp.maximum(m, jnp.max(s[e], axis=0, keepdims=True) + bias[e])
                 scale = jnp.exp2((m_own - m) * EXP2)
-                total = own_sum[g, rows] * scale
-                acc = own_acc[g, rows] * scale
+                total = own_sum[g, :, rows] * scale
+                acc = own_acc[g, :, rows] * scale
                 for e in range(2):
-                    p = jnp.exp2((s[e] - (m - biases[e])) * EXP2)
-                    total = total + jnp.sum(p, axis=1, keepdims=True)
-                    acc = acc + jnp.dot(p.astype(jnp.bfloat16), values[e], preferred_element_type=jnp.float32)
-                result = (acc / total).astype(jnp.bfloat16)
+                    p = jnp.exp2((s[e] - (m - bias[e])) * EXP2)
+                    total = total + jnp.sum(p, axis=0, keepdims=True)
+                    acc = acc + jnp.dot(
+                        values(chosen[e], 0, 4), p.astype(jnp.bfloat16), preferred_element_type=jnp.float32
+                    )
+                result = (acc * (1.0 / total)).T.astype(jnp.bfloat16)
                 to = pl.ds(32 * g, 32)
                 for n, r in enumerate(quarters):
                     for h in range(HEADS):
@@ -440,12 +452,13 @@
         scratch_shapes=[
             pltpu.SMEM((3, 1, BLK), jnp.int32),
             pltpu.VMEM((BLK, HEADS * HD), bf16),
+            pltpu.VMEM((BLK, HD), bf16),
             pltpu.VMEM((BLK // NZ, WIDTH), bf16),
             pltpu.VMEM((2 * NX * NY, 2, BLK, HD), bf16),
             pltpu.VMEM((HEADS * HD, WIDTH), bf16),
-            pltpu.VMEM((4, BLK, HD), f32),
-            pltpu.VMEM((4, BLK, 1), f32),
-            pltpu.VMEM((4, BLK, 1), f32),
+            pltpu.VMEM((4, HD, BLK), f32),
+            pltpu.VMEM((4, 1, BLK), f32),
+            pltpu.VMEM((4, 1, BLK), f32),
             pltpu.VMEM((NY, 128, HEADS * HD), bf16),
             pltpu.VMEM((NY, 128, HEADS * HD), bf16),
             pltpu.VMEM((CHUNKS, NZ, 16, HALF), bf16),

time: 86.3 us -> 85.4 us (0.990)
  Pallas kernels: 84.3 us -> 83.4 us
where the time goes in v3:
time: 85.4 us; the launch traced here: 85.3 us
  Pallas kernels  83.4 us (98%)
  local copies, waits for them, and re-layouts  1.87 us (2%)
    pallas_call x1, Pallas kernels, body(): pl.pallas_call(kernel, out_shape=jax.ShapeDtypeStruct((BLK // NZ, WIDTH),...  83.4 us
    unnamed x1, local copies, waits for them, and re-layouts  1.87 us

profile of v3, /device:TPU:24, one launch (start us, length us, event | category | flops | bytes accessed | tf_op | source)
XLA Modules:
  0.0 85.3 jit_solution(335108374123304209)
XLA Ops:
  0.0 83.4 %attention_mix.1 = bf16[64,4096]{1,0:T(8,128)(2,1)} custom-call(s32[3,1,512]{2,1,0:T(1,128)} %bitcast.13, bf16[512,512]{1,0:T(8,128)(2,1)} %bitcast.9, bf16[512,128]{1,0:T(8,128)(2,1)} %bitcast.11, bf16[512,128]{1,0:T(8,128)(2,1)} %bitcast.12, bf16[512,4096]{1,0:T(8,128)(2,1)} %w_hbm.1, bf16[64,4096]{1,0:T(8,128)(2,1)} %bitcast.10), custom_call_target="tpu_custom_call" | custom-call | tf_op jit(solution)/shard_map/attention_mix/pallas_call | solution.py:447
  83.4 1.9 %copy.8 = bf16[1,1,64,4096]{3,2,1,0:T(8,128)(2,1)} copy(bf16[1,1,64,4096]{3,2,1,0:T(8,128)(2,1)} %bitcast.8) | data formatting | bytes 1048576

commit v4 on v3

--- a/solution.py
+++ b/solution.py
@@ -283,8 +283,11 @@
 
         lax.fori_loop(0, 2, far_pair, 0)
 
+    ways = [core, 1 - core]
+
     def r_copy(n, way, stage, src, dst):
-        return remote(src, dst, r_send.at[n, way, stage], r_recv.at[n, way, stage], up if way == 0 else down)
+        return remote(src, dst, r_send.at[n, way, stage], r_recv.at[n, way, stage],
+                      (c, lax.rem(z + 1 + (NZ - 2) * way, NZ)))
 
     def shard(step):
         return lax.rem(z + step, NZ)
@@ -299,21 +302,22 @@
         columns = pl.ds(pl.multiple_of(h * HALF, HALF), HALF)
         product = jnp.dot(att_in[k], w[:, columns], preferred_element_type=jnp.float32)
         part[n] = product.astype(jnp.bfloat16).reshape(NZ, 16, HALF)
-        r_copy(n, 0, 0, part.at[n, shard(4), :, pl.ds(0, QUART)], rin0.at[n, 0]).start()
-        r_copy(n, 1, 0, part.at[n, shard(4), :, pl.ds(QUART, QUART)], rin0.at[n, 1]).start()
+        for way in ways:
+            columns = pl.ds(pl.multiple_of(way * QUART, QUART), QUART)
+            r_copy(n, way, 0, part.at[n, shard(4), :, columns], rin0.at[n, way]).start()
 
     def stage_1(n):
-        for way, step in ((0, 3), (1, 5)):
-            d = shard(step)
-            columns = pl.ds(way * QUART, QUART)
+        for way in ways:
+            d = shard(3 + 2 * way)
+            columns = pl.ds(pl.multiple_of(way * QUART, QUART), QUART)
             r_copy(n, way, 0, rin0.at[n, way], rin0.at[n, way]).wait_recv()
             total = part[n, d, :, columns].astype(jnp.float32) + rin0[n, way].astype(jnp.float32)
             part[n, d, :, columns] = total.astype(jnp.bfloat16)
             r_copy(n, way, 1, part.at[n, d], rin.at[n, way, 0]).start()
 
     def stage_mid(n, stage):
-        for way, step in ((0, 4 - stage), (1, 4 + stage)):
-            d = shard(step)
+        for way in ways:
+            d = shard(4 - stage + 2 * stage * way)
             r_copy(n, way, stage - 1, rin.at[n, way, stage - 2], rin.at[n, way, stage - 2]).wait_recv()
             total = part[n, d].astype(jnp.float32) + rin[n, way, stage - 2].astype(jnp.float32)
             part[n, d] = total.astype(jnp.bfloat16)

time: 85.4 us -> 85.4 us (level)
  no operation moved by 1% of the time
where the time goes in v4:
time: 85.4 us; the launch traced here: 85.3 us
  Pallas kernels  83.4 us (98%)
  local copies, waits for them, and re-layouts  1.87 us (2%)
    pallas_call x1, Pallas kernels, body(): pl.pallas_call(kernel, out_shape=jax.ShapeDtypeStruct((BLK // NZ, WIDTH),...  83.4 us
    unnamed x1, local copies, waits for them, and re-layouts  1.87 us

profile of v4, /device:TPU:24, one launch (start us, length us, event | category | flops | bytes accessed | tf_op | source)
XLA Modules:
  0.0 85.3 jit_solution(10384463945392502743)
XLA Ops:
  0.0 83.4 %attention_mix.1 = bf16[64,4096]{1,0:T(8,128)(2,1)} custom-call(s32[3,1,512]{2,1,0:T(1,128)} %bitcast.13, bf16[512,512]{1,0:T(8,128)(2,1)} %bitcast.9, bf16[512,128]{1,0:T(8,128)(2,1)} %bitcast.11, bf16[512,128]{1,0:T(8,128)(2,1)} %bitcast.12, bf16[512,4096]{1,0:T(8,128)(2,1)} %w_hbm.1, bf16[64,4096]{1,0:T(8,128)(2,1)} %bitcast.10), custom_call_target="tpu_custom_call" | custom-call | tf_op jit(solution)/shard_map/attention_mix/pallas_call | solution.py:451
  83.4 1.9 %copy.8 = bf16[1,1,64,4096]{3,2,1,0:T(8,128)(2,1)} copy(bf16[1,1,64,4096]{3,2,1,0:T(8,128)(2,1)} %bitcast.8) | data formatting | bytes 1048576

commit v5 on v4

--- a/solution.py
+++ b/solution.py
@@ -21,7 +21,7 @@
 SKEW = 1
 NEG = -1e30
 SHARE_AT = ((2, 1), (3, 2))
-FAR_AT = (-1, -1, 2, 4)
+FAR_AT = (-1, -1, 1, 3)
 EXP2 = math.log2(math.e) / math.sqrt(HD)
 
 

time: 85.4 us -> 85.6 us (level)
  no operation moved by 1% of the time
where the time goes in v5:
time: 85.6 us; the launch traced here: 85.3 us
  Pallas kernels  83.5 us (98%)
  local copies, waits for them, and re-layouts  1.87 us (2%)
    pallas_call x1, Pallas kernels, body(): pl.pallas_call(kernel, out_shape=jax.ShapeDtypeStruct((BLK // NZ, WIDTH),...  83.5 us
    unnamed x1, local copies, waits for them, and re-layouts  1.87 us

profile of v5, /device:TPU:24, one launch (start us, length us, event | category | flops | bytes accessed | tf_op | source)
XLA Modules:
  0.0 85.3 jit_solution(6000591832522475228)
XLA Ops:
  0.0 83.5 %attention_mix.1 = bf16[64,4096]{1,0:T(8,128)(2,1)} custom-call(s32[3,1,512]{2,1,0:T(1,128)} %bitcast.13, bf16[512,512]{1,0:T(8,128)(2,1)} %bitcast.9, bf16[512,128]{1,0:T(8,128)(2,1)} %bitcast.11, bf16[512,128]{1,0:T(8,128)(2,1)} %bitcast.12, bf16[512,4096]{1,0:T(8,128)(2,1)} %w_hbm.1, bf16[64,4096]{1,0:T(8,128)(2,1)} %bitcast.10), custom_call_target="tpu_custom_call" | custom-call | tf_op jit(solution)/shard_map/attention_mix/pallas_call | solution.py:451
  83.5 1.9 %copy.8 = bf16[1,1,64,4096]{3,2,1,0:T(8,128)(2,1)} copy(bf16[1,1,64,4096]{3,2,1,0:T(8,128)(2,1)} %bitcast.8) | data formatting | bytes 1048576
